TPU v7x, 256 devices: a whole 4x4x8 slice. The times are simulated.
256 devices in a mesh: gx: 16 (over y, x), gy: 16 (over z, core).
Axes of the slice: x: 4, y: 4, z: 8, core: 2. Of those that a mesh axis runs over, the one named last changes fastest.
Arguments:
- vectors: float32 [8, 128, 256, 256], P(None, 'gx', 'gy'), may hold values from -10 to 10
- weight_x: float32 [128, 256, 256], P('gx', 'gy'), may hold values from 0.05 to 1
- weight_y: float32 [128, 256, 256], P('gx', 'gy'), may hold values from 0.05 to 1
- weight_z: float32 [128, 256, 256], P('gx', 'gy'), may hold values from 0.05 to 1
Outputs:
- refined: float32 [8, 128, 256, 256], P(None, 'gx', 'gy')
- eigenvalues: float32 [8], replicated
All inputs are finite; a program needn't handle non-finite values.
Results may differ from a plain program's by a relative error of at most 0.000075.
Values sent between devices are 32-bit elements; how exact they have to be, the bound alone decides.
No kernel may reach another device: no remote copies, remote signals or barrier semaphores. Data moves between devices by JAX's collectives and lax.ppermute only.
A program may use at most 128 MiB of HBM per device.

v0:
```python
import jax
import jax.numpy as jnp
from jax import lax
from jax.sharding import PartitionSpec as P

COARSE_SWEEPS = 4
OMEGA = 0.8
SHIFT = 0.1


def shifted(shard, axis, by):
    count = lax.axis_size(axis)
    pairs = [(i, i + by) for i in range(count) if 0 <= i + by < count]
    return lax.ppermute(shard, axis, pairs)


def with_halo(cells, sides, width):
    for axis, dim in sides:
        count = lax.axis_size(axis)
        ends = count - 1
        head = lax.slice_in_dim(cells, 0, width, axis=dim)
        tail = lax.slice_in_dim(cells, cells.shape[dim] - width, cells.shape[dim], axis=dim)
        cells = jnp.concatenate(
            [
                lax.ppermute(tail, axis, [(i, (i + 1) % count) for i in range(ends)]),
                cells,
                lax.ppermute(head, axis, [((i + 1) % count, i) for i in range(ends)]),
            ],
            axis=dim,
        )
    return cells


def lower_x(weights):
    rim = shifted(weights[-1:], "gx", 1)
    return jnp.concatenate([rim, weights[:-1]], 0)


def lower_y(weights):
    rim = shifted(weights[:, -1:], "gy", 1)
    return jnp.concatenate([rim, weights[:, :-1]], 1)


def lower_z(weights):
    return jnp.concatenate([jnp.zeros_like(weights[:, :, :1]), weights[:, :, :-1]], 2)


def trimmed(array):
    return array[..., 1:-1, 1:-1, :]


def inner_sum(field, parts):
    wx, lx, wy, ly, wz, lz = parts
    centre = trimmed(field)
    zpadded = jnp.pad(centre, ((0, 0), (0, 0), (0, 0), (1, 1)))
    total = wx[None] * field[:, 2:, 1:-1] + lx[None] * field[:, :-2, 1:-1]
    total = total + wy[None] * field[:, 1:-1, 2:] + ly[None] * field[:, 1:-1, :-2]
    total = total + wz[None] * zpadded[..., 2:] + lz[None] * zpadded[..., :-2]
    return total


def neighbours(field, parts, level):
    if level == "fine":
        padded = with_halo(field, (("gx", 1), ("gy", 2)), 1)
    else:
        padded = with_halo(field, (("gx", 1), ("gy", 2)), 1)
    return inner_sum(padded, parts)


def jacobi(guess, source, diag, parts, level):
    return (
        guess
        + OMEGA * (source - (diag[None] * guess - neighbours(guess, parts, level))) / diag[None]
    )


def rayleigh_sums(vectors, applied, degree):
    return lax.psum(
        (
            jnp.sum(vectors * applied, axis=(1, 2, 3)),
            jnp.sum(vectors * (degree[None] * vectors), axis=(1, 2, 3)),
        ),
        ("gx", "gy"),
    )


def coarse_weights(wx, wy, wz, degree):
    sx, sy, sz = wx.shape
    shape = (sx // 2, 2, sy // 2, 2, sz // 2, 2)
    cx = wx.reshape(shape)[:, 1].sum(axis=(2, 4))
    cy = wy.reshape(shape)[:, :, :, 1].sum(axis=(1, 4))
    cz = wz.reshape(shape)[..., 1].sum(axis=(1, 3))
    dsum = degree.reshape(shape).sum(axis=(1, 3, 5))
    return (cx, cy, cz, dsum)


def restrict(field):
    kk, sx, sy, sz = field.shape
    return field.reshape(kk, sx // 2, 2, sy // 2, 2, sz // 2, 2).sum(axis=(2, 4, 6))


def prolong(field):
    kk, sx, sy, sz = field.shape
    return jnp.broadcast_to(field[:, :, None, :, None, :, None], (kk, sx, 2, sy, 2, sz, 2)).reshape(
        kk, 2 * sx, 2 * sy, 2 * sz
    )


def per_device(vectors, weight_x, weight_y, weight_z):
    local_x, local_y, depth = weight_x.shape
    span_x = local_x * lax.axis_size("gx")
    span_y = local_y * lax.axis_size("gy")
    pos_x = lax.axis_index("gx") * local_x + lax.broadcasted_iota(jnp.int32, (local_x, 1, 1), 0)
    pos_y = lax.axis_index("gy") * local_y + lax.broadcasted_iota(jnp.int32, (1, local_y, 1), 1)
    pos_z = lax.broadcasted_iota(jnp.int32, (1, 1, depth), 2)
    wx = jnp.where(pos_x < span_x - 1, weight_x, jnp.zeros_like(weight_x))
    wy = jnp.where(pos_y < span_y - 1, weight_y, jnp.zeros_like(weight_y))
    wz = jnp.where(pos_z < depth - 1, weight_z, jnp.zeros_like(weight_z))
    parts = (wx, lower_x(wx), wy, lower_y(wy), wz, lower_z(wz))
    degree = parts[0] + parts[1] + parts[2] + parts[3] + parts[4] + parts[5]
    applied = degree[None] * vectors - neighbours(vectors, parts, "fine")
    numer, denom = rayleigh_sums(vectors, applied, degree)
    eigenvalues = numer / denom
    resid = applied - eigenvalues[:, None, None, None] * (degree[None] * vectors)
    dfine = (1.0 + SHIFT) * degree
    guess = OMEGA * resid / dfine[None]
    guess = jacobi(guess, resid, dfine, parts, "fine")
    fine_rest = resid - (dfine[None] * guess - neighbours(guess, parts, "fine"))
    cx, cy, cz, dsum = coarse_weights(wx, wy, wz, degree)
    cparts = (cx, lower_x(cx), cy, lower_y(cy), cz, lower_z(cz))
    dcoarse = cparts[0] + cparts[1] + cparts[2] + cparts[3] + cparts[4] + cparts[5] + SHIFT * dsum
    rcoarse = restrict(fine_rest)
    correction = OMEGA * rcoarse / dcoarse[None]
    for sweep in range(COARSE_SWEEPS - 1):
        correction = jacobi(correction, rcoarse, dcoarse, cparts, "coarse")
    guess = guess + prolong(correction)
    guess = jacobi(guess, resid, dfine, parts, "fine")
    updated = vectors - guess
    local_gram = jnp.einsum(
        "aijk,bijk->ab", updated, degree[None] * updated, precision=lax.Precision.HIGHEST
    )
    gram = lax.psum(local_gram, ("gx", "gy"))
    gram = gram / (span_x * span_y * depth)
    chol = jnp.linalg.cholesky(gram)
    flat = updated.reshape(updated.shape[0], -1)
    refined = jax.scipy.linalg.solve_triangular(chol, flat, lower=True).reshape(updated.shape)
    return (refined, eigenvalues)


def solution(mesh):
    return jax.shard_map(
        per_device,
        mesh=mesh,
        in_specs=(
            P(None, "gx", "gy", None),
            P("gx", "gy", None),
            P("gx", "gy", None),
            P("gx", "gy", None),
        ),
        out_specs=(P(None, "gx", "gy", None), P()),
        check_vma=False,
    )
```

profile of v0, /device:TPU:1, one launch (start us, length us, event | category | flops | bytes accessed | tf_op | source)
XLA Modules:
  0.0 427.5 jit_solution(8508537190117706973)
XLA Ops:
  6.6 4.4 %collective-permute-start.1 = (f32[8,1,256]{2,1,0:T(1,128)S(1)}, f32[8,1,256]{2,1,0:T(1,128)S(1)}, u32[]{:S(2)}, u32[]{:S(2)}) collective-permute-start(f32[8,1,256]{2,1,0:T(1,128)S(1)} %slice.374), channel_id=1, source_target_pairs={{0,1},{1,2},{2,3},{3,4},{4,5},{5,6},{6,7},{7,8},{8,9},{9,10},{10,1... | collective-permute-start | bytes 24584 | tf_op jit(solution)/shard_map/ppermute | solution.py:14
  16.5 9.8 %reshape.74 = f32[4,2,8,2,128,2]{5,4,3,2,1,0:T(8,128)} reshape(f32[8,16,256]{2,1,0:T(8,128)S(1)} %broadcast_select_fusion.2) | data formatting | bytes 262144 | tf_op jit(solution)/shard_map/reshape | solution.py:90
  35.9 82.2 %all-reduce.9 = (f32[8]{0:T(128)S(1)}, f32[8]{0:T(128)S(1)}) all-reduce(f32[8]{0:T(128)S(1)} %get-tuple-element.19, f32[8]{0:T(128)S(1)} %get-tuple-element.18), channel_id=1, replica_groups=mesh['gx'=16,'gy'=16] {'gx','gy'}, use_global_device_ids=true, to_apply=%region_1.2 | all-reduce | flops 16 | bytes 128 | tf_op jit(solution)/shard_map/psum | solution.py:78
  121.8 4.7 %collective-permute-start.7 = (f32[8,1,16,256]{3,2,1,0:T(8,128)}, f32[8,1,16,256]{3,2,1,0:T(8,128)}, u32[]{:S(2)}, u32[]{:S(2)}) collective-permute-start(f32[8,1,16,256]{3,2,1,0:T(8,128)} %get-tuple-element.44), channel_id=1, source_target_pairs={{0,16},{16,32},{32,48},{48,64},{64,80},{80,96},{96,112},{112,128},... | collective-permute-start | bytes 393224 | tf_op jit(solution)/shard_map/ppermute | solution.py:25
  133.0 9.7 %reshape.75 = f32[4,2,8,2,128,2]{5,4,3,2,1,0:T(8,128)} reshape(f32[8,16,256]{2,1,0:T(8,128)S(1)} %broadcast_select_fusion.1) | data formatting | bytes 262144 | tf_op jit(solution)/shard_map/reshape | solution.py:91
  156.1 9.8 %reshape.76 = f32[4,2,8,2,128,2]{5,4,3,2,1,0:T(8,128)} reshape(f32[8,16,256]{2,1,0:T(8,128)S(1)} %broadcast_select_fusion) | data formatting | bytes 262144 | tf_op jit(solution)/shard_map/reshape | solution.py:92
  166.1 5.3 %fusion.13 = f32[8,8,16,256]{3,2,1,0:T(8,128)S(1)} fusion(f32[8,8,16,256]{3,2,1,0:T(8,128)} %copy-done.1, f32[8,8,16,256]{3,2,1,0:T(8,128)S(1)} %get-tuple-element.27, f32[8,10,1,256]{3,2,1,0:T(1,128)S(1)} %copy.441, f32[8,1,16,256]{3,2,1,0:T(8,128)} %copy-done.25, f32[8,1,16,256]{3,2,1,0:T(8,128)} %collective-permute-done.7, ...), kind=kLoop, calls=%fused_computation.28 | loop fusion | flops 6553600 | bytes 4489216 | tf_op jit(solution)/shard_map/add | solution.py:72
  173.4 4.7 %collective-permute-start.11 = (f32[8,1,16,256]{3,2,1,0:T(8,128)}, f32[8,1,16,256]{3,2,1,0:T(8,128)}, u32[]{:S(2)}, u32[]{:S(2)}) collective-permute-start(f32[8,1,16,256]{3,2,1,0:T(8,128)} %get-tuple-element.42), channel_id=1, source_target_pairs={{0,16},{16,32},{32,48},{48,64},{64,80},{80,96},{96,112},{112,128},... | collective-permute-start | bytes 393224 | tf_op jit(solution)/shard_map/ppermute | solution.py:25
  178.1 6.8 %slice_reduce_fusion = f32[4,8,128]{2,1,0:T(8,128)} fusion(f32[4,2,8,2,128,2]{5,4,3,2,1,0:T(8,128)} %reshape.76), kind=kLoop, calls=%fused_computation | loop fusion | flops 12288 | bytes 81920 | tf_op jit(solution)/shard_map/reduce_sum | solution.py:92
  184.8 10.5 %reshape.77 = f32[4,2,8,2,128,2]{5,4,3,2,1,0:T(8,128)} reshape(f32[8,16,256]{2,1,0:T(8,128)} %copy-done.8) | data formatting | bytes 262144 | tf_op jit(solution)/shard_map/reshape | solution.py:93
  195.3 4.6 %reduce_sum.69 = f32[4,8,128]{2,1,0:T(8,128)} reduce(f32[4,2,8,2,128,2]{5,4,3,2,1,0:T(8,128)} %reshape.77, f32[]{:T(128)} %constant.65.clone.1), dimensions={1,3,5}, to_apply=%region_8.9 | reduce | flops 28672 | bytes 147460 | tf_op jit(solution)/shard_map/reduce_sum | solution.py:93
  211.3 9.8 %copy.446 = f32[8,8,16,256]{0,3,2,1:T(8,128)} copy(f32[8,8,16,256]{3,2,1,0:T(8,128)} %fusion.19) | data formatting | bytes 2097152 | tf_op jit(solution)/shard_map/sub | solution.py:128
  221.1 13.1 %reduce_sum.65 = f32[8,4,8,128]{0,3,2,1:T(8,128)} reduce(f32[8,4,2,8,2,128,2]{0,6,5,4,3,2,1:T(2,128)} %bitcast.30, f32[]{:T(128)} %constant.65.clone.1), dimensions={2,4,6}, to_apply=%region_4.5 | reduce | flops 229376 | bytes 1179652 | tf_op jit(solution)/shard_map/reduce_sum | solution.py:99
  239.4 4.0 collective-permute-start.17
  247.4 4.3 %collective-permute-start.19 = (f32[8,6,1,128]{3,2,1,0:T(1,128)S(1)}, f32[8,6,1,128]{3,2,1,0:T(1,128)S(1)}, u32[]{:S(2)}, u32[]{:S(2)}) collective-permute-start(f32[8,6,1,128]{3,2,1,0:T(1,128)S(1)} %get-tuple-element.53), channel_id=1, source_target_pairs={{0,1},{1,2},{2,3},{3,4},{4,5},{5,6},{6,7},{7,8},{8,9},{9,10},{10,1... | collective-permute-start | bytes 73736 | tf_op jit(solution)/shard_map/ppermute | solution.py:25
  255.1 4.6 %collective-permute-start.21 = (f32[8,1,8,128]{3,2,1,0:T(8,128)S(1)}, f32[8,1,8,128]{3,2,1,0:T(8,128)S(1)}, u32[]{:S(2)}, u32[]{:S(2)}) collective-permute-start(f32[8,1,8,128]{3,2,1,0:T(8,128)S(1)} %get-tuple-element.56), channel_id=1, source_target_pairs={{0,16},{16,32},{32,48},{48,64},{64,80},{80,96},{96,112},{112,128},... | collective-permute-start | bytes 98312 | tf_op jit(solution)/shard_map/ppermute | solution.py:25
  262.6 5.1 %collective-permute-start.23 = (f32[8,6,1,128]{3,2,1,0:T(1,128)S(1)}, f32[8,6,1,128]{3,2,1,0:T(1,128)S(1)}, u32[]{:S(2)}, u32[]{:S(2)}) collective-permute-start(f32[8,6,1,128]{3,2,1,0:T(1,128)S(1)} %get-tuple-element.51), channel_id=1, source_target_pairs={{0,1},{1,2},{2,3},{3,4},{4,5},{5,6},{6,7},{7,8},{8,9},{9,10},{10,1... | collective-permute-start | bytes 73736 | tf_op jit(solution)/shard_map/ppermute | solution.py:25
  270.1 4.6 %collective-permute-start.25 = (f32[8,1,8,128]{3,2,1,0:T(8,128)S(1)}, f32[8,1,8,128]{3,2,1,0:T(8,128)S(1)}, u32[]{:S(2)}, u32[]{:S(2)}) collective-permute-start(f32[8,1,8,128]{3,2,1,0:T(8,128)S(1)} %get-tuple-element.54), channel_id=1, source_target_pairs={{0,16},{16,32},{32,48},{48,64},{64,80},{80,96},{96,112},{112,128},... | collective-permute-start | bytes 98312 | tf_op jit(solution)/shard_map/ppermute | solution.py:25
  277.7 5.1 %collective-permute-start.27 = (f32[8,6,1,128]{3,2,1,0:T(1,128)S(1)}, f32[8,6,1,128]{3,2,1,0:T(1,128)S(1)}, u32[]{:S(2)}, u32[]{:S(2)}) collective-permute-start(f32[8,6,1,128]{3,2,1,0:T(1,128)S(1)} %get-tuple-element.49), channel_id=1, source_target_pairs={{0,1},{1,2},{2,3},{3,4},{4,5},{5,6},{6,7},{7,8},{8,9},{9,10},{10,1... | collective-permute-start | bytes 73736 | tf_op jit(solution)/shard_map/ppermute | solution.py:25
  287.4 7.1 %broadcast_in_dim.30 = f32[8,4,2,8,2,128,2]{0,6,5,4,3,2,1:T(2,128)} broadcast(f32[8,4,8,128]{0,3,2,1:T(8,128)} %copy.451), dimensions={0,1,3,5} | broadcast | bytes 1179648 | tf_op jit(solution)/shard_map/broadcast_in_dim | solution.py:104
  294.5 10.6 %copy.452 = f32[8,8,16,256]{3,2,1,0:T(8,128)} copy(f32[8,8,16,256]{0,3,2,1:T(8,128)} %bitcast.31) | data formatting | bytes 2097152 | tf_op jit(solution)/shard_map/reshape | solution.py:104
  308.1 4.6 %collective-permute-start.29 = (f32[8,1,16,256]{3,2,1,0:T(8,128)S(1)}, f32[8,1,16,256]{3,2,1,0:T(8,128)S(1)}, u32[]{:S(2)}, u32[]{:S(2)}) collective-permute-start(f32[8,1,16,256]{3,2,1,0:T(8,128)S(1)} %get-tuple-element.40), channel_id=1, source_target_pairs={{0,16},{16,32},{32,48},{48,64},{64,80},{80,96},{96,112},{112,128},... | collective-permute-start | bytes 393224 | tf_op jit(solution)/shard_map/ppermute | solution.py:25
  316.7 5.3 %collective-permute-start.31 = (f32[8,10,1,256]{3,0,2,1:T(8,128)S(1)}, f32[8,10,1,256]{3,0,2,1:T(8,128)S(1)}, u32[]{:S(2)}, u32[]{:S(2)}) collective-permute-start(f32[8,10,1,256]{3,0,2,1:T(8,128)S(1)} %copy.455), channel_id=1, source_target_pairs={{0,1},{1,2},{2,3},{3,4},{4,5},{5,6},{6,7},{7,8},{8,9},{9,10},{10,1... | collective-permute-start | bytes 245768 | tf_op jit(solution)/shard_map/ppermute | solution.py:25
  327.9 93.9 %psum.23 = f32[8,8]{0,1:T(8,128)S(1)} all-reduce(f32[8,8]{0,1:T(8,128)S(1)} %convolution_bitcast_fusion), channel_id=1, replica_groups=mesh['gx'=16,'gy'=16] {'gx','gy'}, use_global_device_ids=true, to_apply=%region_9.10 | all-reduce | flops 64 | bytes 512 | tf_op jit(solution)/shard_map/psum | solution.py:142
  (198 shorter events, 101.3 us)
Async XLA Ops:
  1.7 30.6 %collective-permute-start = (f32[1,16,256]{2,1,0:T(8,128)S(1)}, f32[1,16,256]{2,1,0:T(8,128)S(1)}, u32[]{:S(2)}, u32[]{:S(2)}) collective-permute-start(f32[1,16,256]{2,1,0:T(8,128)S(1)} %slice.372), channel_id=1, source_target_pairs={{0,16},{16,32},{32,48},{48,64},{64,80},{80,96},{96,112},{112,128},... | collective-permute-start | bytes 49160 | tf_op jit(solution)/shard_map/ppermute | solution.py:14
  6.6 25.6 %collective-permute-start.1 = (f32[8,1,256]{2,1,0:T(1,128)S(1)}, f32[8,1,256]{2,1,0:T(1,128)S(1)}, u32[]{:S(2)}, u32[]{:S(2)}) collective-permute-start(f32[8,1,256]{2,1,0:T(1,128)S(1)} %slice.374), channel_id=1, source_target_pairs={{0,1},{1,2},{2,3},{3,4},{4,5},{5,6},{6,7},{7,8},{8,9},{9,10},{10,1... | collective-permute-start | bytes 24584 | tf_op jit(solution)/shard_map/ppermute | solution.py:14
  12.0 14.3 %collective-permute-start.3 = (f32[8,1,16,256]{3,2,1,0:T(8,128)S(1)}, f32[8,1,16,256]{3,2,1,0:T(8,128)S(1)}, u32[]{:S(2)}, u32[]{:S(2)}) collective-permute-start(f32[8,1,16,256]{3,2,1,0:T(8,128)S(1)} %get-tuple-element.47), channel_id=1, source_target_pairs={{0,16},{16,32},{32,48},{48,64},{64,80},{80,96},{96,112},{112,128},... | collective-permute-start | bytes 393224 | tf_op jit(solution)/shard_map/ppermute | solution.py:25
  15.2 11.3 %collective-permute-start.2 = (f32[8,1,16,256]{3,2,1,0:T(8,128)S(1)}, f32[8,1,16,256]{3,2,1,0:T(8,128)S(1)}, u32[]{:S(2)}, u32[]{:S(2)}) collective-permute-start(f32[8,1,16,256]{3,2,1,0:T(8,128)S(1)} %get-tuple-element.46), channel_id=1, source_target_pairs={{16,0},{32,16},{48,32},{64,48},{80,64},{96,80},{112,96},{128,112},... | collective-permute-start | bytes 393224 | tf_op jit(solution)/shard_map/ppermute | solution.py:27
  26.6 6.4 %collective-permute-start.4 = (f32[8,10,1,256]{3,0,2,1:T(8,128)S(1)}, f32[8,10,1,256]{3,0,2,1:T(8,128)S(1)}, u32[]{:S(2)}, u32[]{:S(2)}) collective-permute-start(f32[8,10,1,256]{3,0,2,1:T(8,128)S(1)} %copy.466), channel_id=1, source_target_pairs={{1,0},{2,1},{3,2},{4,3},{5,4},{6,5},{7,6},{8,7},{9,8},{10,9},{11,1... | collective-permute-start | bytes 245768 | tf_op jit(solution)/shard_map/ppermute | solution.py:27
  120.6 22.2 %collective-permute-start.6 = (f32[8,1,16,256]{3,2,1,0:T(8,128)}, f32[8,1,16,256]{3,2,1,0:T(8,128)S(1)}, u32[]{:S(2)}, u32[]{:S(2)}) collective-permute-start(f32[8,1,16,256]{3,2,1,0:T(8,128)} %get-tuple-element.45), channel_id=1, source_target_pairs={{16,0},{32,16},{48,32},{64,48},{80,64},{96,80},{112,96},{128,112},... | collective-permute-start | bytes 393224 | tf_op jit(solution)/shard_map/ppermute | solution.py:27
  121.8 20.9 %collective-permute-start.7 = (f32[8,1,16,256]{3,2,1,0:T(8,128)}, f32[8,1,16,256]{3,2,1,0:T(8,128)}, u32[]{:S(2)}, u32[]{:S(2)}) collective-permute-start(f32[8,1,16,256]{3,2,1,0:T(8,128)} %get-tuple-element.44), channel_id=1, source_target_pairs={{0,16},{16,32},{32,48},{48,64},{64,80},{80,96},{96,112},{112,128},... | collective-permute-start | bytes 393224 | tf_op jit(solution)/shard_map/ppermute | solution.py:25
  130.5 76.3 %collective-permute-start.14 = (f32[1,8,128]{2,1,0:T(8,128)}, f32[1,8,128]{2,1,0:T(8,128)}, u32[]{:S(2)}, u32[]{:S(2)}) collective-permute-start(f32[1,8,128]{2,1,0:T(8,128)} %slice.384), channel_id=1, source_target_pairs={{0,16},{16,32},{32,48},{48,64},{64,80},{80,96},{96,112},{112,128},... | collective-permute-start | bytes 12296 | tf_op jit(solution)/shard_map/ppermute | solution.py:14
  143.8 22.1 %collective-permute-start.8 = (f32[8,10,1,256]{3,0,2,1:T(8,128)S(1)}, f32[8,10,1,256]{3,0,2,1:T(8,128)S(1)}, u32[]{:S(2)}, u32[]{:S(2)}) collective-permute-start(f32[8,10,1,256]{3,0,2,1:T(8,128)S(1)} %copy.438), channel_id=1, source_target_pairs={{1,0},{2,1},{3,2},{4,3},{5,4},{6,5},{7,6},{8,7},{9,8},{10,9},{11,1... | collective-permute-start | bytes 245768 | tf_op jit(solution)/shard_map/ppermute | solution.py:27
  147.2 18.7 %collective-permute-start.9 = (f32[8,10,1,256]{3,0,2,1:T(8,128)S(1)}, f32[8,10,1,256]{3,0,2,1:T(8,128)S(1)}, u32[]{:S(2)}, u32[]{:S(2)}) collective-permute-start(f32[8,10,1,256]{3,0,2,1:T(8,128)S(1)} %copy.440), channel_id=1, source_target_pairs={{0,1},{1,2},{2,3},{3,4},{4,5},{5,6},{6,7},{7,8},{8,9},{9,10},{10,1... | collective-permute-start | bytes 245768 | tf_op jit(solution)/shard_map/ppermute | solution.py:25
  153.5 53.3 %collective-permute-start.15 = (f32[4,1,128]{2,1,0:T(1,128)}, f32[4,1,128]{2,1,0:T(1,128)}, u32[]{:S(2)}, u32[]{:S(2)}) collective-permute-start(f32[4,1,128]{2,1,0:T(1,128)} %slice.387), channel_id=1, source_target_pairs={{0,1},{1,2},{2,3},{3,4},{4,5},{5,6},{6,7},{7,8},{8,9},{9,10},{10,1... | collective-permute-start | bytes 6152 | tf_op jit(solution)/shard_map/ppermute | solution.py:14
  172.1 27.9 %collective-permute-start.10 = (f32[8,1,16,256]{3,2,1,0:T(8,128)}, f32[8,1,16,256]{3,2,1,0:T(8,128)}, u32[]{:S(2)}, u32[]{:S(2)}) collective-permute-start(f32[8,1,16,256]{3,2,1,0:T(8,128)} %get-tuple-element.43), channel_id=1, source_target_pairs={{16,0},{32,16},{48,32},{64,48},{80,64},{96,80},{112,96},{128,112},... | collective-permute-start | bytes 393224 | tf_op jit(solution)/shard_map/ppermute | solution.py:27
  173.4 26.6 %collective-permute-start.11 = (f32[8,1,16,256]{3,2,1,0:T(8,128)}, f32[8,1,16,256]{3,2,1,0:T(8,128)}, u32[]{:S(2)}, u32[]{:S(2)}) collective-permute-start(f32[8,1,16,256]{3,2,1,0:T(8,128)} %get-tuple-element.42), channel_id=1, source_target_pairs={{0,16},{16,32},{32,48},{48,64},{64,80},{80,96},{96,112},{112,128},... | collective-permute-start | bytes 393224 | tf_op jit(solution)/shard_map/ppermute | solution.py:25
  201.2 7.0 %collective-permute-start.12 = (f32[8,10,1,256]{3,0,2,1:T(8,128)S(1)}, f32[8,10,1,256]{3,0,2,1:T(8,128)S(1)}, u32[]{:S(2)}, u32[]{:S(2)}) collective-permute-start(f32[8,10,1,256]{3,0,2,1:T(8,128)S(1)} %copy.442), channel_id=1, source_target_pairs={{1,0},{2,1},{3,2},{4,3},{5,4},{6,5},{7,6},{8,7},{9,8},{10,9},{11,1... | collective-permute-start | bytes 245768 | tf_op jit(solution)/shard_map/ppermute | solution.py:27
  244.4 7.3 %collective-permute-start.18 = (f32[8,6,1,128]{3,2,1,0:T(1,128)S(1)}, f32[8,6,1,128]{3,2,1,0:T(1,128)S(1)}, u32[]{:S(2)}, u32[]{:S(2)}) collective-permute-start(f32[8,6,1,128]{3,2,1,0:T(1,128)S(1)} %get-tuple-element.52), channel_id=1, source_target_pairs={{1,0},{2,1},{3,2},{4,3},{5,4},{6,5},{7,6},{8,7},{9,8},{10,9},{11,1... | collective-permute-start | bytes 73736 | tf_op jit(solution)/shard_map/ppermute | solution.py:27
  253.8 5.9 %collective-permute-start.20 = (f32[8,1,8,128]{3,2,1,0:T(8,128)S(1)}, f32[8,1,8,128]{3,2,1,0:T(8,128)S(1)}, u32[]{:S(2)}, u32[]{:S(2)}) collective-permute-start(f32[8,1,8,128]{3,2,1,0:T(8,128)S(1)} %get-tuple-element.57), channel_id=1, source_target_pairs={{16,0},{32,16},{48,32},{64,48},{80,64},{96,80},{112,96},{128,112},... | collective-permute-start | bytes 98312 | tf_op jit(solution)/shard_map/ppermute | solution.py:27
  260.7 7.0 %collective-permute-start.22 = (f32[8,6,1,128]{3,2,1,0:T(1,128)S(1)}, f32[8,6,1,128]{3,2,1,0:T(1,128)S(1)}, u32[]{:S(2)}, u32[]{:S(2)}) collective-permute-start(f32[8,6,1,128]{3,2,1,0:T(1,128)S(1)} %get-tuple-element.50), channel_id=1, source_target_pairs={{1,0},{2,1},{3,2},{4,3},{5,4},{6,5},{7,6},{8,7},{9,8},{10,9},{11,1... | collective-permute-start | bytes 73736 | tf_op jit(solution)/shard_map/ppermute | solution.py:27
  262.6 6.0 %collective-permute-start.23 = (f32[8,6,1,128]{3,2,1,0:T(1,128)S(1)}, f32[8,6,1,128]{3,2,1,0:T(1,128)S(1)}, u32[]{:S(2)}, u32[]{:S(2)}) collective-permute-start(f32[8,6,1,128]{3,2,1,0:T(1,128)S(1)} %get-tuple-element.51), channel_id=1, source_target_pairs={{0,1},{1,2},{2,3},{3,4},{4,5},{5,6},{6,7},{7,8},{8,9},{9,10},{10,1... | collective-permute-start | bytes 73736 | tf_op jit(solution)/shard_map/ppermute | solution.py:25
  275.8 7.0 %collective-permute-start.26 = (f32[8,6,1,128]{3,2,1,0:T(1,128)S(1)}, f32[8,6,1,128]{3,2,1,0:T(1,128)S(1)}, u32[]{:S(2)}, u32[]{:S(2)}) collective-permute-start(f32[8,6,1,128]{3,2,1,0:T(1,128)S(1)} %get-tuple-element.48), channel_id=1, source_target_pairs={{1,0},{2,1},{3,2},{4,3},{5,4},{6,5},{7,6},{8,7},{9,8},{10,9},{11,1... | collective-permute-start | bytes 73736 | tf_op jit(solution)/shard_map/ppermute | solution.py:27
  277.7 6.0 %collective-permute-start.27 = (f32[8,6,1,128]{3,2,1,0:T(1,128)S(1)}, f32[8,6,1,128]{3,2,1,0:T(1,128)S(1)}, u32[]{:S(2)}, u32[]{:S(2)}) collective-permute-start(f32[8,6,1,128]{3,2,1,0:T(1,128)S(1)} %get-tuple-element.49), channel_id=1, source_target_pairs={{0,1},{1,2},{2,3},{3,4},{4,5},{5,6},{6,7},{7,8},{8,9},{9,10},{10,1... | collective-permute-start | bytes 73736 | tf_op jit(solution)/shard_map/ppermute | solution.py:25
  306.6 6.5 %collective-permute-start.28 = (f32[8,1,16,256]{3,2,1,0:T(8,128)S(1)}, f32[8,1,16,256]{3,2,1,0:T(8,128)S(1)}, u32[]{:S(2)}, u32[]{:S(2)}) collective-permute-start(f32[8,1,16,256]{3,2,1,0:T(8,128)S(1)} %get-tuple-element.41), channel_id=1, source_target_pairs={{16,0},{32,16},{48,32},{64,48},{80,64},{96,80},{112,96},{128,112},... | collective-permute-start | bytes 393224 | tf_op jit(solution)/shard_map/ppermute | solution.py:27
  308.1 6.5 %collective-permute-start.29 = (f32[8,1,16,256]{3,2,1,0:T(8,128)S(1)}, f32[8,1,16,256]{3,2,1,0:T(8,128)S(1)}, u32[]{:S(2)}, u32[]{:S(2)}) collective-permute-start(f32[8,1,16,256]{3,2,1,0:T(8,128)S(1)} %get-tuple-element.40), channel_id=1, source_target_pairs={{0,16},{16,32},{32,48},{48,64},{64,80},{80,96},{96,112},{112,128},... | collective-permute-start | bytes 393224 | tf_op jit(solution)/shard_map/ppermute | solution.py:25
  314.7 7.2 %collective-permute-start.30 = (f32[8,10,1,256]{3,0,2,1:T(8,128)S(1)}, f32[8,10,1,256]{3,0,2,1:T(8,128)S(1)}, u32[]{:S(2)}, u32[]{:S(2)}) collective-permute-start(f32[8,10,1,256]{3,0,2,1:T(8,128)S(1)} %copy.453), channel_id=1, source_target_pairs={{1,0},{2,1},{3,2},{4,3},{5,4},{6,5},{7,6},{8,7},{9,8},{10,9},{11,1... | collective-permute-start | bytes 245768 | tf_op jit(solution)/shard_map/ppermute | solution.py:27
  316.7 6.5 %collective-permute-start.31 = (f32[8,10,1,256]{3,0,2,1:T(8,128)S(1)}, f32[8,10,1,256]{3,0,2,1:T(8,128)S(1)}, u32[]{:S(2)}, u32[]{:S(2)}) collective-permute-start(f32[8,10,1,256]{3,0,2,1:T(8,128)S(1)} %copy.455), channel_id=1, source_target_pairs={{0,1},{1,2},{2,3},{3,4},{4,5},{5,6},{6,7},{7,8},{8,9},{9,10},{10,1... | collective-permute-start | bytes 245768 | tf_op jit(solution)/shard_map/ppermute | solution.py:25
  (45 other events, 621.3 us)
where the time goes:
time: 429 us; the launch traced here: 427 us
  blocking collectives  176 us (41%)
  starting transfers between devices  98.6 us (23%)
  local copies, waits for them, and re-layouts  80.4 us (19%)
  other arithmetic  57.3 us (13%)
  waiting for transfers between devices  9.35 us (2%)
    psum x1, blocking collectives, per_device(): gram = lax.psum(local_gram, ('gx', 'gy'))  93.9 us
    psum x1, blocking collectives, rayleigh_sums(): lax.psum((jnp.sum(vectors * applied, axis=(1, 2, 3)), jnp.sum(vectors * (...  82.2 us
    ppermute x14, starting transfers between devices, with_halo(): lax.ppermute(tail, axis, [(i, (i + 1) % count) for i in range(ends)])  59 us
    ppermute x14, starting transfers between devices, with_halo(): lax.ppermute(head, axis, [((i + 1) % count, i) for i in range(ends)])  26.2 us
    ppermute x4, starting transfers between devices, shifted(): return lax.ppermute(shard, axis, pairs)  13.3 us
    reduce_sum x1, other arithmetic, restrict(): field.reshape(kk, sx // 2, 2, sy // 2, 2, sz // 2, 2).sum(axis=(2, 4, 6))  13.1 us
    reshape x1, local copies, waits for them, and re-layouts, prolong(): jnp.broadcast_to(field[:, :, None, :, None, :, None], (kk, sx, 2, sy, 2,...  10.6 us
    reshape x1, local copies, waits for them, and re-layouts, coarse_weights(): dsum = degree.reshape(shape).sum(axis=(1, 3, 5))  10.5 us
  transfers between devices with their start and end apart: 32, of which 10 were waited for; matrix products, arithmetic and copies ran while one was open for 17% of the time, Pallas kernels for 0%

commit v1 on v0

--- a/solution.py
+++ b/solution.py
@@ -2,6 +2,7 @@
 import jax.numpy as jnp
 from jax import lax
 from jax.sharding import PartitionSpec as P
+from jax.lax import psum
 
 COARSE_SWEEPS = 4
 OMEGA = 0.8
@@ -75,12 +76,15 @@
 
 
 def rayleigh_sums(vectors, applied, degree):
-    return lax.psum(
-        (
-            jnp.sum(vectors * applied, axis=(1, 2, 3)),
-            jnp.sum(vectors * (degree[None] * vectors), axis=(1, 2, 3)),
+    return psum(
+        psum(
+            (
+                jnp.sum(vectors * applied, axis=(1, 2, 3)),
+                jnp.sum(vectors * (degree[None] * vectors), axis=(1, 2, 3)),
+            ),
+            "gx",
         ),
-        ("gx", "gy"),
+        "gy",
     )
 
 

time: 429 us -> 411 us (0.958)
  blocking collectives: 176 us -> 159 us
    psum x1 -> x2, blocking collectives: 82.2 us -> 67.1 us  [the longest x1 34 us: rayleigh_sums(): psum(psum((jnp.sum(vectors * applied, axis=(1, 2, 3)), jnp.sum(vectors *...]
where the time goes in v1:
time: 411 us; the launch traced here: 409 us
  blocking collectives  159 us (39%)
  starting transfers between devices  97.2 us (24%)
  local copies, waits for them, and re-layouts  80.5 us (20%)
  other arithmetic  57.4 us (14%)
  waiting for transfers between devices  9.34 us (2%)
    psum x1, blocking collectives, per_device(): gram = lax.psum(local_gram, ('gx', 'gy'))  92.2 us
    ppermute x14, starting transfers between devices, with_halo(): lax.ppermute(tail, axis, [(i, (i + 1) % count) for i in range(ends)])  58.6 us
    psum x1, blocking collectives, rayleigh_sums(): psum(psum((jnp.sum(vectors * applied, axis=(1, 2, 3)), jnp.sum(vectors *...  34 us
    psum x1, blocking collectives, rayleigh_sums(): psum((jnp.sum(vectors * applied, axis=(1, 2, 3)), jnp.sum(vectors * (degr...  33.1 us
    ppermute x14, starting transfers between devices, with_halo(): lax.ppermute(head, axis, [((i + 1) % count, i) for i in range(ends)])  26.4 us
    reduce_sum x1, other arithmetic, restrict(): field.reshape(kk, sx // 2, 2, sy // 2, 2, sz // 2, 2).sum(axis=(2, 4, 6))  13.1 us
    ppermute x4, starting transfers between devices, shifted(): return lax.ppermute(shard, axis, pairs)  12.2 us
    reshape x1, local copies, waits for them, and re-layouts, prolong(): jnp.broadcast_to(field[:, :, None, :, None, :, None], (kk, sx, 2, sy, 2,...  10.6 us
  transfers between devices with their start and end apart: 32, of which 10 were waited for; matrix products, arithmetic and copies ran while one was open for 17% of the time, Pallas kernels for 0%

profile of v1, /device:TPU:1, one launch (start us, length us, event | category | flops | bytes accessed | tf_op | source)
XLA Modules:
  0.0 409.5 jit_solution(4294703556194932448)
XLA Ops:
  6.6 4.4 %collective-permute-start.1 = (f32[8,1,256]{2,1,0:T(1,128)S(1)}, f32[8,1,256]{2,1,0:T(1,128)S(1)}, u32[]{:S(2)}, u32[]{:S(2)}) collective-permute-start(f32[8,1,256]{2,1,0:T(1,128)S(1)} %slice.374), channel_id=1, source_target_pairs={{0,1},{1,2},{2,3},{3,4},{4,5},{5,6},{6,7},{7,8},{8,9},{9,10},{10,1... | collective-permute-start | bytes 24584 | tf_op jit(solution)/shard_map/ppermute | solution.py:15
  16.5 9.8 %reshape.74 = f32[4,2,8,2,128,2]{5,4,3,2,1,0:T(8,128)} reshape(f32[8,16,256]{2,1,0:T(8,128)S(1)} %broadcast_select_fusion.2) | data formatting | bytes 262144 | tf_op jit(solution)/shard_map/reshape | solution.py:94
  35.9 33.1 %all-reduce.10 = (f32[8]{0:T(128)S(1)}, f32[8]{0:T(128)S(1)}) all-reduce(f32[8]{0:T(128)S(1)} %get-tuple-element.19, f32[8]{0:T(128)S(1)} %get-tuple-element.18), channel_id=1, replica_groups=mesh['gx'=16,'gy'=16] {'gx'}, use_global_device_ids=true, to_apply=%region_1.2 | all-reduce | flops 16 | bytes 128 | tf_op jit(solution)/shard_map/psum | solution.py:80
  69.0 34.0 %all-reduce.9 = (f32[8]{0:T(128)S(1)}, f32[8]{0:T(128)S(1)}) all-reduce(f32[8]{0:T(128)S(1)} %get-tuple-element.22, f32[8]{0:T(128)S(1)} %get-tuple-element.23), channel_id=1, replica_groups=mesh['gx'=16,'gy'=16] {'gy'}, use_global_device_ids=true, to_apply=%region_2.3 | all-reduce | flops 16 | bytes 128 | tf_op jit(solution)/shard_map/psum | solution.py:79
  106.8 4.6 %collective-permute-start.7 = (f32[8,1,16,256]{3,2,1,0:T(8,128)}, f32[8,1,16,256]{3,2,1,0:T(8,128)}, u32[]{:S(2)}, u32[]{:S(2)}) collective-permute-start(f32[8,1,16,256]{3,2,1,0:T(8,128)} %get-tuple-element.46), channel_id=1, source_target_pairs={{0,16},{16,32},{32,48},{48,64},{64,80},{80,96},{96,112},{112,128},... | collective-permute-start | bytes 393224 | tf_op jit(solution)/shard_map/ppermute | solution.py:26
  117.3 9.8 %reshape.75 = f32[4,2,8,2,128,2]{5,4,3,2,1,0:T(8,128)} reshape(f32[8,16,256]{2,1,0:T(8,128)S(1)} %broadcast_select_fusion.1) | data formatting | bytes 262144 | tf_op jit(solution)/shard_map/reshape | solution.py:95
  139.2 9.8 %reshape.76 = f32[4,2,8,2,128,2]{5,4,3,2,1,0:T(8,128)} reshape(f32[8,16,256]{2,1,0:T(8,128)S(1)} %broadcast_select_fusion) | data formatting | bytes 262144 | tf_op jit(solution)/shard_map/reshape | solution.py:96
  149.2 5.3 %fusion.13 = f32[8,8,16,256]{3,2,1,0:T(8,128)S(1)} fusion(f32[8,8,16,256]{3,2,1,0:T(8,128)} %copy-done.1, f32[8,8,16,256]{3,2,1,0:T(8,128)S(1)} %get-tuple-element.29, f32[8,10,1,256]{3,2,1,0:T(1,128)S(1)} %copy.441, f32[8,1,16,256]{3,2,1,0:T(8,128)} %copy-done.25, f32[8,1,16,256]{3,2,1,0:T(8,128)} %collective-permute-done.7, ...), kind=kLoop, calls=%fused_computation.28 | loop fusion | flops 6553600 | bytes 4489216 | tf_op jit(solution)/shard_map/add | solution.py:73
  156.5 4.6 %collective-permute-start.11 = (f32[8,1,16,256]{3,2,1,0:T(8,128)}, f32[8,1,16,256]{3,2,1,0:T(8,128)}, u32[]{:S(2)}, u32[]{:S(2)}) collective-permute-start(f32[8,1,16,256]{3,2,1,0:T(8,128)} %get-tuple-element.44), channel_id=1, source_target_pairs={{0,16},{16,32},{32,48},{48,64},{64,80},{80,96},{96,112},{112,128},... | collective-permute-start | bytes 393224 | tf_op jit(solution)/shard_map/ppermute | solution.py:26
  161.2 6.8 %slice_reduce_fusion = f32[4,8,128]{2,1,0:T(8,128)} fusion(f32[4,2,8,2,128,2]{5,4,3,2,1,0:T(8,128)} %reshape.76), kind=kLoop, calls=%fused_computation | loop fusion | flops 12288 | bytes 81920 | tf_op jit(solution)/shard_map/reduce_sum | solution.py:96
  167.9 10.5 %reshape.77 = f32[4,2,8,2,128,2]{5,4,3,2,1,0:T(8,128)} reshape(f32[8,16,256]{2,1,0:T(8,128)} %copy-done.8) | data formatting | bytes 262144 | tf_op jit(solution)/shard_map/reshape | solution.py:97
  178.5 4.6 %reduce_sum.69 = f32[4,8,128]{2,1,0:T(8,128)} reduce(f32[4,2,8,2,128,2]{5,4,3,2,1,0:T(8,128)} %reshape.77, f32[]{:T(128)} %constant.65.clone.1), dimensions={1,3,5}, to_apply=%region_10.11 | reduce | flops 28672 | bytes 147460 | tf_op jit(solution)/shard_map/reduce_sum | solution.py:97
  194.4 9.8 %copy.446 = f32[8,8,16,256]{0,3,2,1:T(8,128)} copy(f32[8,8,16,256]{3,2,1,0:T(8,128)} %fusion.19) | data formatting | bytes 2097152 | tf_op jit(solution)/shard_map/sub | solution.py:132
  204.3 13.1 %reduce_sum.65 = f32[8,4,8,128]{0,3,2,1:T(8,128)} reduce(f32[8,4,2,8,2,128,2]{0,6,5,4,3,2,1:T(2,128)} %bitcast.30, f32[]{:T(128)} %constant.65.clone.1), dimensions={2,4,6}, to_apply=%region_6.7 | reduce | flops 229376 | bytes 1179652 | tf_op jit(solution)/shard_map/reduce_sum | solution.py:103
  222.6 4.0 collective-permute-start.17
  238.2 4.6 %collective-permute-start.21 = (f32[8,1,8,128]{3,2,1,0:T(8,128)S(1)}, f32[8,1,8,128]{3,2,1,0:T(8,128)S(1)}, u32[]{:S(2)}, u32[]{:S(2)}) collective-permute-start(f32[8,1,8,128]{3,2,1,0:T(8,128)S(1)} %get-tuple-element.58), channel_id=1, source_target_pairs={{0,16},{16,32},{32,48},{48,64},{64,80},{80,96},{96,112},{112,128},... | collective-permute-start | bytes 98312 | tf_op jit(solution)/shard_map/ppermute | solution.py:26
  245.8 5.1 %collective-permute-start.23 = (f32[8,6,1,128]{3,2,1,0:T(1,128)S(1)}, f32[8,6,1,128]{3,2,1,0:T(1,128)S(1)}, u32[]{:S(2)}, u32[]{:S(2)}) collective-permute-start(f32[8,6,1,128]{3,2,1,0:T(1,128)S(1)} %get-tuple-element.53), channel_id=1, source_target_pairs={{0,1},{1,2},{2,3},{3,4},{4,5},{5,6},{6,7},{7,8},{8,9},{9,10},{10,1... | collective-permute-start | bytes 73736 | tf_op jit(solution)/shard_map/ppermute | solution.py:26
  253.3 4.6 %collective-permute-start.25 = (f32[8,1,8,128]{3,2,1,0:T(8,128)S(1)}, f32[8,1,8,128]{3,2,1,0:T(8,128)S(1)}, u32[]{:S(2)}, u32[]{:S(2)}) collective-permute-start(f32[8,1,8,128]{3,2,1,0:T(8,128)S(1)} %get-tuple-element.56), channel_id=1, source_target_pairs={{0,16},{16,32},{32,48},{48,64},{64,80},{80,96},{96,112},{112,128},... | collective-permute-start | bytes 98312 | tf_op jit(solution)/shard_map/ppermute | solution.py:26
  260.8 5.1 %collective-permute-start.27 = (f32[8,6,1,128]{3,2,1,0:T(1,128)S(1)}, f32[8,6,1,128]{3,2,1,0:T(1,128)S(1)}, u32[]{:S(2)}, u32[]{:S(2)}) collective-permute-start(f32[8,6,1,128]{3,2,1,0:T(1,128)S(1)} %get-tuple-element.51), channel_id=1, source_target_pairs={{0,1},{1,2},{2,3},{3,4},{4,5},{5,6},{6,7},{7,8},{8,9},{9,10},{10,1... | collective-permute-start | bytes 73736 | tf_op jit(solution)/shard_map/ppermute | solution.py:26
  270.5 7.1 %broadcast_in_dim.30 = f32[8,4,2,8,2,128,2]{0,6,5,4,3,2,1:T(2,128)} broadcast(f32[8,4,8,128]{0,3,2,1:T(8,128)} %copy.451), dimensions={0,1,3,5} | broadcast | bytes 1179648 | tf_op jit(solution)/shard_map/broadcast_in_dim | solution.py:108
  277.7 10.6 %copy.452 = f32[8,8,16,256]{3,2,1,0:T(8,128)} copy(f32[8,8,16,256]{0,3,2,1:T(8,128)} %bitcast.31) | data formatting | bytes 2097152 | tf_op jit(solution)/shard_map/reshape | solution.py:108
  291.2 4.6 %collective-permute-start.29 = (f32[8,1,16,256]{3,2,1,0:T(8,128)S(1)}, f32[8,1,16,256]{3,2,1,0:T(8,128)S(1)}, u32[]{:S(2)}, u32[]{:S(2)}) collective-permute-start(f32[8,1,16,256]{3,2,1,0:T(8,128)S(1)} %get-tuple-element.42), channel_id=1, source_target_pairs={{0,16},{16,32},{32,48},{48,64},{64,80},{80,96},{96,112},{112,128},... | collective-permute-start | bytes 393224 | tf_op jit(solution)/shard_map/ppermute | solution.py:26
  299.8 5.8 %collective-permute-start.31 = (f32[8,10,1,256]{3,0,2,1:T(8,128)S(1)}, f32[8,10,1,256]{3,0,2,1:T(8,128)S(1)}, u32[]{:S(2)}, u32[]{:S(2)}) collective-permute-start(f32[8,10,1,256]{3,0,2,1:T(8,128)S(1)} %copy.455), channel_id=1, source_target_pairs={{0,1},{1,2},{2,3},{3,4},{4,5},{5,6},{6,7},{7,8},{8,9},{9,10},{10,1... | collective-permute-start | bytes 245768 | tf_op jit(solution)/shard_map/ppermute | solution.py:26
  311.6 92.2 %psum.39 = f32[8,8]{0,1:T(8,128)S(1)} all-reduce(f32[8,8]{0,1:T(8,128)S(1)} %convolution_bitcast_fusion), channel_id=1, replica_groups=mesh['gx'=16,'gy'=16] {'gx','gy'}, use_global_device_ids=true, to_apply=%region_11.12 | all-reduce | flops 64 | bytes 512 | tf_op jit(solution)/shard_map/psum | solution.py:146
  (199 shorter events, 103.8 us)
Async XLA Ops:
  1.7 30.6 %collective-permute-start = (f32[1,16,256]{2,1,0:T(8,128)S(1)}, f32[1,16,256]{2,1,0:T(8,128)S(1)}, u32[]{:S(2)}, u32[]{:S(2)}) collective-permute-start(f32[1,16,256]{2,1,0:T(8,128)S(1)} %slice.372), channel_id=1, source_target_pairs={{0,16},{16,32},{32,48},{48,64},{64,80},{80,96},{96,112},{112,128},... | collective-permute-start | bytes 49160 | tf_op jit(solution)/shard_map/ppermute | solution.py:15
  6.6 25.6 %collective-permute-start.1 = (f32[8,1,256]{2,1,0:T(1,128)S(1)}, f32[8,1,256]{2,1,0:T(1,128)S(1)}, u32[]{:S(2)}, u32[]{:S(2)}) collective-permute-start(f32[8,1,256]{2,1,0:T(1,128)S(1)} %slice.374), channel_id=1, source_target_pairs={{0,1},{1,2},{2,3},{3,4},{4,5},{5,6},{6,7},{7,8},{8,9},{9,10},{10,1... | collective-permute-start | bytes 24584 | tf_op jit(solution)/shard_map/ppermute | solution.py:15
  12.0 14.3 %collective-permute-start.3 = (f32[8,1,16,256]{3,2,1,0:T(8,128)S(1)}, f32[8,1,16,256]{3,2,1,0:T(8,128)S(1)}, u32[]{:S(2)}, u32[]{:S(2)}) collective-permute-start(f32[8,1,16,256]{3,2,1,0:T(8,128)S(1)} %get-tuple-element.49), channel_id=1, source_target_pairs={{0,16},{16,32},{32,48},{48,64},{64,80},{80,96},{96,112},{112,128},... | collective-permute-start | bytes 393224 | tf_op jit(solution)/shard_map/ppermute | solution.py:26
  15.2 11.3 %collective-permute-start.2 = (f32[8,1,16,256]{3,2,1,0:T(8,128)S(1)}, f32[8,1,16,256]{3,2,1,0:T(8,128)S(1)}, u32[]{:S(2)}, u32[]{:S(2)}) collective-permute-start(f32[8,1,16,256]{3,2,1,0:T(8,128)S(1)} %get-tuple-element.48), channel_id=1, source_target_pairs={{16,0},{32,16},{48,32},{64,48},{80,64},{96,80},{112,96},{128,112},... | collective-permute-start | bytes 393224 | tf_op jit(solution)/shard_map/ppermute | solution.py:28
  26.6 6.5 %collective-permute-start.4 = (f32[8,10,1,256]{3,0,2,1:T(8,128)S(1)}, f32[8,10,1,256]{3,0,2,1:T(8,128)S(1)}, u32[]{:S(2)}, u32[]{:S(2)}) collective-permute-start(f32[8,10,1,256]{3,0,2,1:T(8,128)S(1)} %copy.466), channel_id=1, source_target_pairs={{1,0},{2,1},{3,2},{4,3},{5,4},{6,5},{7,6},{8,7},{9,8},{10,9},{11,1... | collective-permute-start | bytes 245768 | tf_op jit(solution)/shard_map/ppermute | solution.py:28
  105.5 21.6 %collective-permute-start.6 = (f32[8,1,16,256]{3,2,1,0:T(8,128)}, f32[8,1,16,256]{3,2,1,0:T(8,128)S(1)}, u32[]{:S(2)}, u32[]{:S(2)}) collective-permute-start(f32[8,1,16,256]{3,2,1,0:T(8,128)} %get-tuple-element.47), channel_id=1, source_target_pairs={{16,0},{32,16},{48,32},{64,48},{80,64},{96,80},{112,96},{128,112},... | collective-permute-start | bytes 393224 | tf_op jit(solution)/shard_map/ppermute | solution.py:28
  106.8 20.3 %collective-permute-start.7 = (f32[8,1,16,256]{3,2,1,0:T(8,128)}, f32[8,1,16,256]{3,2,1,0:T(8,128)}, u32[]{:S(2)}, u32[]{:S(2)}) collective-permute-start(f32[8,1,16,256]{3,2,1,0:T(8,128)} %get-tuple-element.46), channel_id=1, source_target_pairs={{0,16},{16,32},{32,48},{48,64},{64,80},{80,96},{96,112},{112,128},... | collective-permute-start | bytes 393224 | tf_op jit(solution)/shard_map/ppermute | solution.py:26
  115.4 74.5 %collective-permute-start.14 = (f32[1,8,128]{2,1,0:T(8,128)}, f32[1,8,128]{2,1,0:T(8,128)}, u32[]{:S(2)}, u32[]{:S(2)}) collective-permute-start(f32[1,8,128]{2,1,0:T(8,128)} %slice.384), channel_id=1, source_target_pairs={{0,16},{16,32},{32,48},{48,64},{64,80},{80,96},{96,112},{112,128},... | collective-permute-start | bytes 12296 | tf_op jit(solution)/shard_map/ppermute | solution.py:15
  128.1 20.8 %collective-permute-start.8 = (f32[8,10,1,256]{3,0,2,1:T(8,128)S(1)}, f32[8,10,1,256]{3,0,2,1:T(8,128)S(1)}, u32[]{:S(2)}, u32[]{:S(2)}) collective-permute-start(f32[8,10,1,256]{3,0,2,1:T(8,128)S(1)} %copy.438), channel_id=1, source_target_pairs={{1,0},{2,1},{3,2},{4,3},{5,4},{6,5},{7,6},{8,7},{9,8},{10,9},{11,1... | collective-permute-start | bytes 245768 | tf_op jit(solution)/shard_map/ppermute | solution.py:28
  130.8 18.3 %collective-permute-start.9 = (f32[8,10,1,256]{3,0,2,1:T(8,128)S(1)}, f32[8,10,1,256]{3,0,2,1:T(8,128)S(1)}, u32[]{:S(2)}, u32[]{:S(2)}) collective-permute-start(f32[8,10,1,256]{3,0,2,1:T(8,128)S(1)} %copy.440), channel_id=1, source_target_pairs={{0,1},{1,2},{2,3},{3,4},{4,5},{5,6},{6,7},{7,8},{8,9},{9,10},{10,1... | collective-permute-start | bytes 245768 | tf_op jit(solution)/shard_map/ppermute | solution.py:26
  137.1 52.8 %collective-permute-start.15 = (f32[4,1,128]{2,1,0:T(1,128)}, f32[4,1,128]{2,1,0:T(1,128)}, u32[]{:S(2)}, u32[]{:S(2)}) collective-permute-start(f32[4,1,128]{2,1,0:T(1,128)} %slice.387), channel_id=1, source_target_pairs={{0,1},{1,2},{2,3},{3,4},{4,5},{5,6},{6,7},{7,8},{8,9},{9,10},{10,1... | collective-permute-start | bytes 6152 | tf_op jit(solution)/shard_map/ppermute | solution.py:15
  155.2 27.9 %collective-permute-start.10 = (f32[8,1,16,256]{3,2,1,0:T(8,128)}, f32[8,1,16,256]{3,2,1,0:T(8,128)}, u32[]{:S(2)}, u32[]{:S(2)}) collective-permute-start(f32[8,1,16,256]{3,2,1,0:T(8,128)} %get-tuple-element.45), channel_id=1, source_target_pairs={{16,0},{32,16},{48,32},{64,48},{80,64},{96,80},{112,96},{128,112},... | collective-permute-start | bytes 393224 | tf_op jit(solution)/shard_map/ppermute | solution.py:28
  156.5 26.6 %collective-permute-start.11 = (f32[8,1,16,256]{3,2,1,0:T(8,128)}, f32[8,1,16,256]{3,2,1,0:T(8,128)}, u32[]{:S(2)}, u32[]{:S(2)}) collective-permute-start(f32[8,1,16,256]{3,2,1,0:T(8,128)} %get-tuple-element.44), channel_id=1, source_target_pairs={{0,16},{16,32},{32,48},{48,64},{64,80},{80,96},{96,112},{112,128},... | collective-permute-start | bytes 393224 | tf_op jit(solution)/shard_map/ppermute | solution.py:26
  184.3 7.0 %collective-permute-start.12 = (f32[8,10,1,256]{3,0,2,1:T(8,128)S(1)}, f32[8,10,1,256]{3,0,2,1:T(8,128)S(1)}, u32[]{:S(2)}, u32[]{:S(2)}) collective-permute-start(f32[8,10,1,256]{3,0,2,1:T(8,128)S(1)} %copy.442), channel_id=1, source_target_pairs={{1,0},{2,1},{3,2},{4,3},{5,4},{6,5},{7,6},{8,7},{9,8},{10,9},{11,1... | collective-permute-start | bytes 245768 | tf_op jit(solution)/shard_map/ppermute | solution.py:28
  227.6 7.3 %collective-permute-start.18 = (f32[8,6,1,128]{3,2,1,0:T(1,128)S(1)}, f32[8,6,1,128]{3,2,1,0:T(1,128)S(1)}, u32[]{:S(2)}, u32[]{:S(2)}) collective-permute-start(f32[8,6,1,128]{3,2,1,0:T(1,128)S(1)} %get-tuple-element.54), channel_id=1, source_target_pairs={{1,0},{2,1},{3,2},{4,3},{5,4},{6,5},{7,6},{8,7},{9,8},{10,9},{11,1... | collective-permute-start | bytes 73736 | tf_op jit(solution)/shard_map/ppermute | solution.py:28
  236.9 5.9 %collective-permute-start.20 = (f32[8,1,8,128]{3,2,1,0:T(8,128)S(1)}, f32[8,1,8,128]{3,2,1,0:T(8,128)S(1)}, u32[]{:S(2)}, u32[]{:S(2)}) collective-permute-start(f32[8,1,8,128]{3,2,1,0:T(8,128)S(1)} %get-tuple-element.59), channel_id=1, source_target_pairs={{16,0},{32,16},{48,32},{64,48},{80,64},{96,80},{112,96},{128,112},... | collective-permute-start | bytes 98312 | tf_op jit(solution)/shard_map/ppermute | solution.py:28
  243.9 7.0 %collective-permute-start.22 = (f32[8,6,1,128]{3,2,1,0:T(1,128)S(1)}, f32[8,6,1,128]{3,2,1,0:T(1,128)S(1)}, u32[]{:S(2)}, u32[]{:S(2)}) collective-permute-start(f32[8,6,1,128]{3,2,1,0:T(1,128)S(1)} %get-tuple-element.52), channel_id=1, source_target_pairs={{1,0},{2,1},{3,2},{4,3},{5,4},{6,5},{7,6},{8,7},{9,8},{10,9},{11,1... | collective-permute-start | bytes 73736 | tf_op jit(solution)/shard_map/ppermute | solution.py:28
  245.8 6.0 %collective-permute-start.23 = (f32[8,6,1,128]{3,2,1,0:T(1,128)S(1)}, f32[8,6,1,128]{3,2,1,0:T(1,128)S(1)}, u32[]{:S(2)}, u32[]{:S(2)}) collective-permute-start(f32[8,6,1,128]{3,2,1,0:T(1,128)S(1)} %get-tuple-element.53), channel_id=1, source_target_pairs={{0,1},{1,2},{2,3},{3,4},{4,5},{5,6},{6,7},{7,8},{8,9},{9,10},{10,1... | collective-permute-start | bytes 73736 | tf_op jit(solution)/shard_map/ppermute | solution.py:26
  258.9 7.0 %collective-permute-start.26 = (f32[8,6,1,128]{3,2,1,0:T(1,128)S(1)}, f32[8,6,1,128]{3,2,1,0:T(1,128)S(1)}, u32[]{:S(2)}, u32[]{:S(2)}) collective-permute-start(f32[8,6,1,128]{3,2,1,0:T(1,128)S(1)} %get-tuple-element.50), channel_id=1, source_target_pairs={{1,0},{2,1},{3,2},{4,3},{5,4},{6,5},{7,6},{8,7},{9,8},{10,9},{11,1... | collective-permute-start | bytes 73736 | tf_op jit(solution)/shard_map/ppermute | solution.py:28
  260.8 6.0 %collective-permute-start.27 = (f32[8,6,1,128]{3,2,1,0:T(1,128)S(1)}, f32[8,6,1,128]{3,2,1,0:T(1,128)S(1)}, u32[]{:S(2)}, u32[]{:S(2)}) collective-permute-start(f32[8,6,1,128]{3,2,1,0:T(1,128)S(1)} %get-tuple-element.51), channel_id=1, source_target_pairs={{0,1},{1,2},{2,3},{3,4},{4,5},{5,6},{6,7},{7,8},{8,9},{9,10},{10,1... | collective-permute-start | bytes 73736 | tf_op jit(solution)/shard_map/ppermute | solution.py:26
  289.8 6.4 %collective-permute-start.28 = (f32[8,1,16,256]{3,2,1,0:T(8,128)S(1)}, f32[8,1,16,256]{3,2,1,0:T(8,128)S(1)}, u32[]{:S(2)}, u32[]{:S(2)}) collective-permute-start(f32[8,1,16,256]{3,2,1,0:T(8,128)S(1)} %get-tuple-element.43), channel_id=1, source_target_pairs={{16,0},{32,16},{48,32},{64,48},{80,64},{96,80},{112,96},{128,112},... | collective-permute-start | bytes 393224 | tf_op jit(solution)/shard_map/ppermute | solution.py:28
  291.2 6.5 %collective-permute-start.29 = (f32[8,1,16,256]{3,2,1,0:T(8,128)S(1)}, f32[8,1,16,256]{3,2,1,0:T(8,128)S(1)}, u32[]{:S(2)}, u32[]{:S(2)}) collective-permute-start(f32[8,1,16,256]{3,2,1,0:T(8,128)S(1)} %get-tuple-element.42), channel_id=1, source_target_pairs={{0,16},{16,32},{32,48},{48,64},{64,80},{80,96},{96,112},{112,128},... | collective-permute-start | bytes 393224 | tf_op jit(solution)/shard_map/ppermute | solution.py:26
  297.9 7.8 %collective-permute-start.30 = (f32[8,10,1,256]{3,0,2,1:T(8,128)S(1)}, f32[8,10,1,256]{3,0,2,1:T(8,128)S(1)}, u32[]{:S(2)}, u32[]{:S(2)}) collective-permute-start(f32[8,10,1,256]{3,0,2,1:T(8,128)S(1)} %copy.453), channel_id=1, source_target_pairs={{1,0},{2,1},{3,2},{4,3},{5,4},{6,5},{7,6},{8,7},{9,8},{10,9},{11,1... | collective-permute-start | bytes 245768 | tf_op jit(solution)/shard_map/ppermute | solution.py:28
  299.8 7.1 %collective-permute-start.31 = (f32[8,10,1,256]{3,0,2,1:T(8,128)S(1)}, f32[8,10,1,256]{3,0,2,1:T(8,128)S(1)}, u32[]{:S(2)}, u32[]{:S(2)}) collective-permute-start(f32[8,10,1,256]{3,0,2,1:T(8,128)S(1)} %copy.455), channel_id=1, source_target_pairs={{0,1},{1,2},{2,3},{3,4},{4,5},{5,6},{6,7},{7,8},{8,9},{9,10},{10,1... | collective-permute-start | bytes 245768 | tf_op jit(solution)/shard_map/ppermute | solution.py:26
  (45 other events, 606.0 us)
